TPU v7x, 32 devices: a whole 2x2x4 slice. The times are simulated.
32 devices in a mesh: tm: 8 (over y, x, core), head: 4 (over z).
Axes of the slice: x: 2, y: 2, z: 4, core: 2. Of those that a mesh axis runs over, the one named last changes fastest.
Arguments:
- queries: bfloat16 [1024, 2048], P(('tm', 'head')), may hold values from -120 to 120
- keys: bfloat16 [1024, 2048], P(('tm', 'head')), may hold values from -5 to 5
- values: bfloat16 [1024, 2048], P(('tm', 'head'))
- history: bfloat16 [8, 4, 32, 512], P('tm'), may hold values from -6 to 6
- fine_proj: bfloat16 [512, 4096], P(None, 'head'), may hold values from -0.25 to 0.25
- coarse_proj: bfloat16 [4096, 4096], P(None, 'head'), may hold values from -0.09375 to 0.09375
- frame_counts: int32 [8], replicated, may hold values from 1 to 4, as said below
- levels: int32 [8], replicated, may hold values from 0 to 1, as said below
Outputs:
- attended: bfloat16 [1024, 2048], P(('tm', 'head'))
Inputs may be any that keep to these rules, and one draw needn't show every extreme that they name: `frame_counts`: some group with level 0 holds all 4 frames. `levels`: both kernels occur.
All inputs are finite; a program needn't handle non-finite values.
Results may differ from a plain program's by a relative error of at most 0.0073.
Values may be sent and summed in bfloat16 or wider, within the bound.
A program may use at most 128 MiB of HBM per device.

v0:
```python
import math

import jax
import jax.numpy as jnp
from jax import lax
from jax.sharding import PartitionSpec as P

HD = 128
HEADS = 16


very_low = -1e30


def masked_frames(history, counts):
    frames = history.shape[1]
    live = jnp.arange(frames, dtype=jnp.int32)[None, :] < counts[:, None]
    return jnp.where(live[:, :, None, None], history, jnp.zeros((), history.dtype))


def fine_only(masked, fine_proj):
    groups, frames, rows, merged = masked.shape
    channels = fine_proj.shape[0] // 32
    columns = merged // channels
    fine = masked.reshape(groups, frames // 2, 2, rows // 4, 4, columns // 4, 4, channels)
    fine = fine.transpose(0, 1, 3, 5, 2, 4, 6, 7).reshape(-1, 32 * channels)
    fine_pairs = jnp.dot(fine, fine_proj, preferred_element_type=jnp.float32).astype(jnp.bfloat16)
    slots = frames // 2 * (rows // 4) * (columns // 4)
    return fine_pairs.reshape(groups, slots, fine_proj.shape[1])


def coarse_only(masked, coarse_proj):
    groups, frames, rows, merged = masked.shape
    channels = coarse_proj.shape[0] // 256
    columns = merged // channels
    coarse = masked.reshape(groups, 4, rows // 8, 8, columns // 8, 8, channels)
    coarse = coarse.transpose(0, 2, 4, 1, 3, 5, 6).reshape(-1, 256 * channels)
    coarse_pairs = jnp.dot(coarse, coarse_proj, preferred_element_type=jnp.float32).astype(
        jnp.bfloat16
    )
    slots = frames // 2 * (rows // 4) * (columns // 4)
    coarse_count = rows // 8 * (columns // 8)
    width = coarse_proj.shape[1]
    coarse_pairs = coarse_pairs.reshape(groups, coarse_count, width)
    padding = jnp.zeros((groups, slots - coarse_count, width), jnp.bfloat16)
    return jnp.concatenate([coarse_pairs, padding], axis=1)


def patch_selected(history, counts, levels, fine_proj, coarse_proj):

    def one_group(operands):
        latents, count, level = operands
        masked = masked_frames(latents[None], jnp.reshape(count, (1,)))

        def fine_branch(block):
            return fine_only(block, fine_proj)[0]

        def coarse_branch(block):
            return coarse_only(block, coarse_proj)[0]

        return lax.cond(level == 0, fine_branch, coarse_branch, masked)

    return lax.map(one_group, (history, counts, levels))


def slot_valid(counts, levels, slots):
    index = jnp.arange(slots, dtype=jnp.int32)[None, :]
    fine_live = 2 * (index // (slots // 2)) < counts[:, None]
    coarse_live = index < slots // 8
    return jnp.where(levels[:, None] == 0, fine_live, coarse_live)


def lookup(table, group_ids):
    places = jnp.arange(table.shape[0], dtype=jnp.int32)[None, :]
    return jnp.sum(jnp.where(places == group_ids[:, None], table[None, :], 0), axis=1)


def group_tokens(history, fine_proj, coarse_proj, frame_counts, levels):
    own_group = jnp.reshape(lax.axis_index("tm"), (1,))
    return patch_selected(
        history, lookup(frame_counts, own_group), lookup(levels, own_group), fine_proj, coarse_proj
    )


def start_state(per_device, query_rows):
    return (
        jnp.full((per_device, query_rows), very_low, jnp.float32),
        jnp.zeros((per_device, query_rows), jnp.float32),
        jnp.zeros((per_device, query_rows, HD), jnp.float32),
    )


def absorb(running, query_cube, pair_rows, usable):
    top_run, total, accum = running
    scores = jnp.einsum(
        "qhd,rhd->hqr", query_cube, pair_rows[:, :, :HD], preferred_element_type=jnp.float32
    )
    scores = scores * (1.0 / math.sqrt(HD))
    masked = jnp.where(usable[None, None, :], scores, very_low)
    new_top = jnp.maximum(top_run, jnp.max(masked, axis=2))
    expo = jnp.where(usable[None, None, :], jnp.exp(masked - new_top[:, :, None]), 0.0)
    factor = jnp.exp(top_run - new_top)
    total = total * factor + jnp.sum(expo, axis=2)
    update = jnp.einsum(
        "hqr,rhd->hqd",
        expo.astype(jnp.bfloat16),
        pair_rows[:, :, HD:],
        preferred_element_type=jnp.float32,
    )
    return (new_top, total, accum * factor[:, :, None] + update)


def absorb_blocks(running, query_cube, pair_rows, usable):
    length = pair_rows.shape[0]
    block = math.gcd(length, 1024)
    steps_count = length // block
    stacked = pair_rows.reshape(steps_count, block, pair_rows.shape[1], pair_rows.shape[2])
    masks = usable.reshape(steps_count, block)

    def one_step(state, operands):
        return (absorb(state, query_cube, operands[0], operands[1]), None)

    running, unused = lax.scan(one_step, running, (stacked, masks))
    return running


def body(queries, keys, values, history, fine_proj, coarse_proj, frame_counts, levels):
    tokens_here, width = queries.shape
    pairs = jnp.stack(
        [keys.reshape(tokens_here, HEADS, HD), values.reshape(tokens_here, HEADS, HD)], axis=2
    )
    pairs = pairs.reshape(tokens_here, 2 * width)
    local_queries, local_pairs = (
        lax.all_to_all(queries, "head", split_axis=1, concat_axis=0, tiled=True),
        lax.all_to_all(pairs, "head", split_axis=1, concat_axis=0, tiled=True),
    )
    query_rows = local_queries.shape[0]
    per_device = local_queries.shape[1] // HD
    query_cube = local_queries.reshape(query_rows, per_device, HD)
    running = start_state(per_device, query_rows)
    own_pairs = group_tokens(history, fine_proj, coarse_proj, frame_counts, levels)
    slots = own_pairs.shape[1]
    packed = jnp.concatenate([local_pairs, own_pairs[0]], axis=0)[None]
    piece = lax.all_gather(packed, "tm", axis=0, tiled=True)
    shards = piece.shape[0]
    group_ids = jnp.arange(shards, dtype=jnp.int32)
    hist_live = slot_valid(lookup(frame_counts, group_ids), lookup(levels, group_ids), slots)
    usable = jnp.concatenate(
        [jnp.ones((shards, query_rows), jnp.bool_), hist_live], axis=1
    ).reshape(-1)
    running = absorb_blocks(running, query_cube, piece.reshape(-1, per_device, 2 * HD), usable)
    top_run, total, accum = running
    result = (
        (accum / total[:, :, None])
        .transpose(1, 0, 2)
        .reshape(query_rows, per_device * HD)
        .astype(jnp.bfloat16)
    )
    return lax.all_to_all(result, "head", split_axis=0, concat_axis=1, tiled=True)


def solution(mesh):
    in_specs = (
        P(("tm", "head"), None),
        P(("tm", "head"), None),
        P(("tm", "head"), None),
        P("tm", None, None, None),
        P(None, "head"),
        P(None, "head"),
        P(),
        P(),
    )
    out_specs = P(("tm", "head"), None)
    return jax.shard_map(body, mesh=mesh, in_specs=in_specs, out_specs=out_specs, check_vma=False)
```

profile of v0, /device:TPU:0, one launch (start us, length us, event | category | flops | bytes accessed | tf_op | source)
XLA Modules:
  0.0 103.3 jit_solution(9148300529142718010)
XLA Ops:
  6.5 0.0 copy-start.4
  6.5 0.0 copy-start.3
  6.5 0.0 copy-start.1
  6.5 0.0 copy-start
  6.5 1.2 %stack_reshape.8 = bf16[32,16,1,128]{3,2,1,0:T(2,128)(2,1)S(1)} reshape(bf16[32,2048]{1,0:T(8,128)(2,1)} %param.13) | data formatting | bytes 262144 | tf_op jit(solution)/shard_map/stack;reshape | solution.py:129
  7.8 1.1 %stack_reshape.9 = bf16[32,16,1,128]{3,2,1,0:T(2,128)(2,1)S(1)} reshape(bf16[32,2048]{1,0:T(8,128)(2,1)} %param.14) | data formatting | bytes 262144 | tf_op jit(solution)/shard_map/stack;reshape | solution.py:129
  8.9 0.6 pad_maximum_fusion.1
  9.5 0.1 all_to_all.38
  9.5 0.8 copy.48
  10.3 6.3 %all-to-all-start = ((bf16[32,4,1024]{2,0,1:T(8,128)(2,1)}), bf16[32,4,1024]{2,0,1:T(8,128)(2,1)S(1)}, u32[]{:S(2)}, u32[]{:S(2)}) async-start(bf16[32,4,1024]{2,0,1:T(8,128)(2,1)} %copy.48), calls=%async_computation | async-start | bytes 524288 | tf_op jit(solution)/shard_map/all_to_all | solution.py:135
  16.6 0.0 all-gather.3.cloned.1.call-start
  16.6 0.0 copy-done.4
  16.6 0.0 copy-done.3
  16.7 0.7 fusion.21
  18.0 0.6 iota_compare_fusion.1
  18.6 0.0 copy-done.1
  18.6 0.1 broadcast_select_fusion
  18.7 0.0 copy-done
  18.7 0.0 copy-start.2
  18.8 7.5 %conditional.1 = (bf16[128,1024]{1,0:T(8,128)(2,1)S(1)}) conditional(s32[]{:T(128)} %convert_element_type.23, (bf16[1,4,32,512]{3,2,1,0:T(8,128)(2,1)S(1)}, bf16[4096,1024]{1,0:T(8,128)(2,1)}) %tuple.17, (bf16[1,4,32,512]{3,2,1,0:T(8,128)(2,1)S(1)}, bf16[512,1024]{1,0:T(8,128)(2,1)S(1)}) %tuple.50), branch_computations={%region_2.3_spmd, %region_3.4_spmd} | conditional | flops 134348800 | bytes 9633800 | solution.py:61
  18.8 0.8 reshape.109
  19.6 0.3 copy.62
  19.9 1.8 %reshape.110 = bf16[16,4096]{1,0:T(8,128)(2,1)S(1)} reshape(bf16[1,4,4,4,8,8,16]{6,5,4,3,2,1,0:T(8,128)(2,1)S(1)} %bitcast.61) | data formatting | bytes 262144 | tf_op jit(solution)/shard_map/while/body/eval_jaxpr/cond/branch_0_fun/reshape | solution.py:37
  21.7 4.6 %fusion = bf16[1,16,1024]{2,1,0:T(8,128)(2,1)S(1)} fusion(bf16[16,4096]{1,0:T(8,128)(2,1)S(1)} %reshape.110, bf16[4096,1024]{1,0:T(8,128)(2,1)} %get-tuple-element.83), kind=kOutput, calls=%fused_computation.1 | convolution fusion | flops 134234112 | bytes 8552448 | tf_op jit(solution)/shard_map/while/body/eval_jaxpr/cond/branch_0_fun/dot_general | solution.py:38
  26.3 0.0 all-to-all-done
  26.3 0.8 pad_maximum_fusion
  27.1 0.0 all-gather.3.cloned.1.call-update
  27.2 0.0 copy-done.2
  27.2 0.7 copy.65
  27.8 5.1 %all-to-all-start.1 = ((bf16[32,4,512]{2,0,1:T(8,128)(2,1)}), bf16[32,4,512]{2,0,1:T(8,128)(2,1)S(1)}, u32[]{:S(2)}, u32[]{:S(2)}) async-start(bf16[32,4,512]{2,0,1:T(8,128)(2,1)} %bitcast.48), calls=%async_computation.1 | async-start | bytes 262144 | tf_op jit(solution)/shard_map/all_to_all | solution.py:134
  32.9 0.1 select_reduce_fusion
  33.1 0.1 select_reduce_fusion.1
  33.2 0.1 compare_select_fusion
  33.3 5.6 %all-to-all-done.1 = bf16[32,4,512]{2,0,1:T(8,128)(2,1)S(1)} async-done(((bf16[32,4,512]{2,0,1:T(8,128)(2,1)}), bf16[32,4,512]{2,0,1:T(8,128)(2,1)S(1)}, u32[]{:S(2)}, u32[]{:S(2)}) %all-to-all-start.1) | async-done | bytes 131104 | tf_op jit(solution)/shard_map/all_to_all | solution.py:134
  38.9 26.6 %all-gather.3.cloned.1.call-done = bf16[2048,1024]{1,0:T(8,128)(2,1)} async-done(((bf16[256,1024]{1,0:T(8,128)(2,1)}), bf16[2048,1024]{1,0:T(8,128)(2,1)}) %all-gather.3.cloned.1.call-update) | async-done | bytes 4194320 | tf_op jit(solution)/shard_map/all_gather | solution.py:144
  65.5 7.8 %reshape_reshape.7 = bf16[2,1024,4,256]{3,2,1,0:T(4,128)(2,1)} reshape(bf16[2048,1024]{1,0:T(8,128)(2,1)} %all-gather.3.cloned.1.call-done) | data formatting | bytes 8388608 | tf_op jit(solution)/shard_map/reshape;reshape | solution.py:117
  73.3 11.4 %while.5 = (s32[]{:T(128)}, f32[4,128]{1,0:T(4,128)S(1)}, f32[4,128]{1,0:T(4,128)S(1)}, f32[4,128,128]{2,1,0:T(8,128)S(1)}, pred[2,1024]{1,0:T(4,128)(4,1)S(1)},...) while((s32[]{:T(128)}, f32[4,128]{1,0:T(4,128)S(1)}, ...), condition=%wide.region_9.10_spmd.clone, body=%wide.region_6.9_spmd.clone.sunk | while | flops 275450368 | bytes 17471608 | solution.py:123
  73.4 2.3 %constant_dynamic-slice_fusion.2 = bf16[1,1024,4,256]{3,2,1,0:T(4,128)(2,1)S(1)} fusion(bf16[2,1024,4,256]{3,2,1,0:T(4,128)(2,1)} %get-tuple-element.232, s32[]{:T(128)S(6)} %copy.74), kind=kLoop, calls=%fused_computation.30.clone.1 | loop fusion | bytes 4194308 | tf_op jit(solution)/shard_map/while/body/jit(dynamic_index_in_dim)/dynamic_slice | solution.py:123
  75.7 0.3 copy.67
  76.0 0.8 bitcast_reduce_fusion.2
  76.8 0.9 fusion.36
  77.7 1.3 %convolution_add_fusion.2 = f32[4,128,128]{2,1,0:T(8,128)S(1)} fusion(f32[4,1024,128]{2,1,0:T(8,128)S(1)} %get-tuple-element.206, bf16[1024,4,256]{2,0,1:T(8,128)(2,1)S(1)} %bitcast.60, f32[4,128]{1,0:T(4,128)S(1)} %select_maximum_fusion.2, pred[1024]{0:T(1024)(128)(4,1)S(1)} %dynamic-slice_reduce_fusion.2, ...), kind=kOutput, calls=%fused_computation.14.clone.1 | convolution fusion | flops 137035776 | bytes 3676161 | tf_op jit(solution)/shard_map/while/body/eval_jaxpr/hqr,rhd->hqd/dot_general | solution.py:104
  79.1 2.3 %constant_dynamic-slice_fusion.2 = bf16[1,1024,4,256]{3,2,1,0:T(4,128)(2,1)S(1)} fusion(bf16[2,1024,4,256]{3,2,1,0:T(4,128)(2,1)} %get-tuple-element.232, s32[]{:T(128)S(6)} %copy.74), kind=kLoop, calls=%fused_computation.30.clone.1 | loop fusion | bytes 4194308 | tf_op jit(solution)/shard_map/while/body/jit(dynamic_index_in_dim)/dynamic_slice | solution.py:123
  81.4 0.3 copy.67
  81.7 0.8 bitcast_reduce_fusion.2
  82.5 0.9 fusion.36
  83.4 1.3 %convolution_add_fusion.2 = f32[4,128,128]{2,1,0:T(8,128)S(1)} fusion(f32[4,1024,128]{2,1,0:T(8,128)S(1)} %get-tuple-element.206, bf16[1024,4,256]{2,0,1:T(8,128)(2,1)S(1)} %bitcast.60, f32[4,128]{1,0:T(4,128)S(1)} %select_maximum_fusion.2, pred[1024]{0:T(1024)(128)(4,1)S(1)} %dynamic-slice_reduce_fusion.2, ...), kind=kOutput, calls=%fused_computation.14.clone.1 | convolution fusion | flops 137035776 | bytes 3676161 | tf_op jit(solution)/shard_map/while/body/eval_jaxpr/hqr,rhd->hqd/dot_general | solution.py:104
  84.7 0.1 fusion.19
  84.9 0.1 copy.52
  85.0 0.1 convert_element_type.26
  85.0 10.7 %all_to_all.51 = bf16[4,32,512]{2,1,0:T(8,128)(2,1)S(1)} all-to-all(bf16[4,32,512]{2,1,0:T(8,128)(2,1)S(1)} %convert_element_type.26), channel_id=1, replica_groups=mesh['tm'=8,'head'=4] {'head'}, dimensions={0} | all-to-all | bytes 262144 | tf_op jit(solution)/shard_map/all_to_all | solution.py:159
  95.8 0.7 copy.57
  (19 shorter events, 0.2 us)
Async XLA Ops:
  6.5 10.1 %copy-start.4 = (s32[8]{0:T(128)S(1)}, s32[8]{0:T(128)}, u32[]{:S(2)}) copy-start(s32[8]{0:T(128)} %param.19) | copy-start | bytes 100
  6.5 10.1 %copy-start.3 = (s32[8]{0:T(128)S(1)}, s32[8]{0:T(128)}, u32[]{:S(2)}) copy-start(s32[8]{0:T(128)} %param.18) | copy-start | bytes 100
  6.5 12.1 %copy-start.1 = (bf16[1,4,32,512]{3,2,1,0:T(8,128)(2,1)S(1)}, bf16[1,4,32,512]{3,2,1,0:T(8,128)(2,1)}, u32[]{:S(2)}) copy-start(bf16[1,4,32,512]{3,2,1,0:T(8,128)(2,1)} %param.15) | copy-start | bytes 393220
  6.5 12.2 %copy-start = (bf16[512,1024]{1,0:T(8,128)(2,1)S(1)}, bf16[512,1024]{1,0:T(8,128)(2,1)}, u32[]{:S(2)}) copy-start(bf16[512,1024]{1,0:T(8,128)(2,1)} %param.16) | copy-start | bytes 3145732
  10.3 16.0 %all-to-all-start = ((bf16[32,4,1024]{2,0,1:T(8,128)(2,1)}), bf16[32,4,1024]{2,0,1:T(8,128)(2,1)S(1)}, u32[]{:S(2)}, u32[]{:S(2)}) async-start(bf16[32,4,1024]{2,0,1:T(8,128)(2,1)} %copy.48), calls=%async_computation | async-start | bytes 524288 | tf_op jit(solution)/shard_map/all_to_all | solution.py:135
  16.6 48.9 %all-gather.3.cloned.1.call-start = ((), (), s32[]{:S(2)}) async-start(), calls=%async_computation.3 | async-start | bytes 4718592 | tf_op jit(solution)/shard_map/all_gather | solution.py:144
  18.7 8.4 %copy-start.2 = (bf16[32,2048]{1,0:T(8,128)(2,1)S(1)}, bf16[32,2048]{1,0:T(8,128)(2,1)}, u32[]{:S(2)}) copy-start(bf16[32,2048]{1,0:T(8,128)(2,1)} %param.12) | copy-start | bytes 393220
  27.8 11.0 %all-to-all-start.1 = ((bf16[32,4,512]{2,0,1:T(8,128)(2,1)}), bf16[32,4,512]{2,0,1:T(8,128)(2,1)S(1)}, u32[]{:S(2)}, u32[]{:S(2)}) async-start(bf16[32,4,512]{2,0,1:T(8,128)(2,1)} %bitcast.48), calls=%async_computation.1 | async-start | bytes 262144 | tf_op jit(solution)/shard_map/all_to_all | solution.py:134
Sparse Core Ops, SparseCore 0:
  27.3 38.1 all-gather.2
where the time goes:
time: 103 us
  waiting for transfers between devices  32.2 us (31%)
  local copies, waits for them, and re-layouts  20.7 us (20%)
  between operations  14.2 us (14%)
  starting transfers between devices  11.4 us (11%)
  blocking collectives  10.7 us (10%)
  matrix products  8.81 us (9%)
  other arithmetic  5.1 us (5%)
    all_gather x1, waiting for transfers between devices, body(): piece = lax.all_gather(packed, 'tm', axis=0, tiled=True)  26.6 us
    all_to_all x1, blocking collectives, body(): lax.all_to_all(result, 'head', split_axis=0, concat_axis=1, tiled=True)  10.7 us
    another operation x1, local copies, waits for them, and re-layouts, absorb_blocks(): pair_rows.reshape(steps_count, block, pair_rows.shape[1], pair_rows.shape...  7.84 us
    all_to_all x1, starting transfers between devices, body(): lax.all_to_all(pairs, 'head', split_axis=1, concat_axis=0, tiled=True)  6.32 us
    all_to_all x1, waiting for transfers between devices, body(): lax.all_to_all(queries, 'head', split_axis=1, concat_axis=0, tiled=True)  5.55 us
    dynamic_slice x6, local copies, waits for them, and re-layouts, absorb_blocks(): running, unused = lax.scan(one_step, running, (stacked, masks))  5.24 us
    all_to_all x1, starting transfers between devices, body(): lax.all_to_all(queries, 'head', split_axis=1, concat_axis=0, tiled=True)  5.09 us
    dot_general x1, matrix products, coarse_only(): jnp.dot(coarse, coarse_proj, preferred_element_type=jnp.float32)  4.58 us
  transfers between devices with their start and end apart: 3, of which 2 were waited for; matrix products, arithmetic and copies ran while one was open for 10% of the time, Pallas kernels for 0%

commit v1 on v0

v1 whole, which is shorter than its diff:
```python
import functools
import math

import jax
import jax.numpy as jnp
from jax import lax
from jax.experimental import pallas as pl
from jax.experimental.pallas import tpu as pltpu
from jax.sharding import PartitionSpec as P

HD = 128
HEADS = 16
FRAMES = 4
ROWS = 32
LANES = 512
SLOTS = 128
COARSE = 16
KCHUNKS = 4
QBLOCK = 256

very_low = -1e30
LOG2E = 1.4426950408889634
MESH = pl.DeviceIdType.MESH


def loop(count, step):
    if count <= 4:
        for index in range(count):
            step(index)
    else:

        def one(index, carry):
            step(index)
            return carry

        lax.fori_loop(0, count, one, 0)


def kernel(
    nz,
    tm,
    q_ref,
    k_ref,
    v_ref,
    h_ref,
    fw_ref,
    cw_ref,
    cnt_ref,
    lev_ref,
    out_ref,
    qbuf,
    kvbuf,
    hist,
    hp,
    hv,
    h32,
    p32,
    w2,
    cw,
    res,
    obuf,
    m_ref,
    l_ref,
    acc_ref,
    send_sem,
    recv_sem,
    own_sem,
    fsend,
    frecv,
    hsend,
    hrecv,
    gsend,
    grecv,
    osend,
    orecv,
    wsem,
    fsem,
    hsem,
):
    local = q_ref.shape[0]
    per_plane = HEADS // nz
    sibs = tm // per_plane
    t = lax.axis_index("tm")
    z = lax.axis_index("head")
    j = lax.div(t, sibs)
    s = lax.rem(t, sibs)
    me = z * per_plane + j
    kdepth = cw.shape[0] // KCHUNKS

    hist_load = pltpu.make_async_copy(h_ref.at[0], hv, hsem)
    hist_load.start()
    fine_loads = []
    for i in range(8):
        for half in range(2):
            fine_loads.append(
                pltpu.make_async_copy(
                    fw_ref.at[pl.ds(i * 64, 64)],
                    w2.at[pl.ds(i * 128 + half * 64, 64)],
                    fsem.at[i, half],
                )
            )
    coarse_loads = [
        pltpu.make_async_copy(
            cw_ref.at[pl.ds(i * kdepth, kdepth)], cw.at[pl.ds(i * kdepth, kdepth)], wsem.at[i]
        )
        for i in range(KCHUNKS)
    ]

    def device(head, sib):
        plane = lax.div(head, per_plane)
        return (lax.rem(head, per_plane) * sibs + sib, plane)

    z_order = sorted(range(nz), key=lambda d: -min(d, nz - d))
    peers = []
    for dz in z_order:
        for dj in range(per_plane):
            if dz or dj:
                pz = lax.rem(z + dz, nz)
                peers.append((dz, pz * per_plane + lax.rem(j + dj, per_plane)))

    def sib_of(d):
        return lax.rem(s + 1 + d, sibs)

    barrier = pltpu.get_barrier_semaphore()
    for _, p in peers:
        pl.semaphore_signal(barrier, inc=1, device_id=device(p, s), device_id_type=MESH)

    def greet(d):
        pl.semaphore_signal(barrier, inc=1, device_id=device(me, sib_of(d)), device_id_type=MESH)

    loop(sibs - 1, greet)
    for load in fine_loads:
        load.start()
    for load in coarse_loads:
        load.start()
    pl.semaphore_wait(barrier, HEADS - 1 + sibs - 1)

    def columns(head):
        return pl.ds(pl.multiple_of(head * HD, HD), HD)

    def rows_of(head):
        return pl.ds(pl.multiple_of(head * local, local), local)

    def targets(row):
        return (
            qbuf.at[rows_of(row)],
            kvbuf.at[s, rows_of(row), pl.ds(0, HD)],
            kvbuf.at[s, rows_of(row), pl.ds(HD, HD)],
        )

    def qkv(p):
        return [
            pltpu.make_async_remote_copy(
                src_ref=src.at[:, columns(p)],
                dst_ref=dst,
                send_sem=send_sem.at[p, n],
                recv_sem=recv_sem.at[me, n],
                device_id=device(p, s),
                device_id_type=MESH,
            )
            for n, (src, dst) in enumerate(zip((q_ref, k_ref, v_ref), targets(me)))
        ]

    def qkv_in(p):
        return [
            pltpu.make_async_remote_copy(
                src_ref=src.at[:, columns(p)],
                dst_ref=dst,
                send_sem=send_sem.at[p, n],
                recv_sem=recv_sem.at[p, n],
                device_id=device(p, s),
                device_id_type=MESH,
            )
            for n, (src, dst) in enumerate(zip((q_ref, k_ref, v_ref), targets(p)))
        ]

    for _, p in peers:
        for copy in qkv(p):
            copy.start()
    own = [
        pltpu.make_async_copy(src.at[:, columns(me)], dst, own_sem.at[n])
        for n, (src, dst) in enumerate(zip((q_ref, k_ref, v_ref), targets(me)))
    ]
    for copy in own:
        copy.start()

    count = cnt_ref[t]
    level = lev_ref[t]
    hist_load.wait()
    blocks = LANES // HD
    for f in range(FRAMES):
        for cb in range(blocks):
            piece = hv[f, :, cb * HD : (cb + 1) * HD].astype(jnp.float32)
            h32[f, cb] = jnp.where(f < count, piece, 0.0)
    for f in range(FRAMES):
        for r in range(8):
            for cb in range(blocks):
                p32[cb * 4 : cb * 4 + 4, (f * 8 + r) * HD : (f * 8 + r + 1) * HD] = h32[
                    f, cb, pl.ds(r, 4, stride=8)
                ]
    lane_low = lax.broadcasted_iota(jnp.int32, (32, HD), 1) < HD // 2
    parts = []
    for ff in range(2):
        for r in range(4):
            stack = []
            for big in range(2):
                x = jnp.concatenate(
                    [
                        h32[big * 2 + ff, cb, pl.ds(r, 8, stride=4)]
                        for cb in range(blocks)
                    ],
                    axis=0,
                )
                stack.append(jnp.where(lane_low, x, 0.0))
                stack.append(jnp.where(lane_low, 0.0, x))
            parts.append(jnp.concatenate(stack, axis=0).astype(jnp.bfloat16))
    fine_in = jnp.concatenate(parts, axis=1)
    for load in fine_loads:
        load.wait()
    for jj in range(per_plane):
        h_cols = slice(jj * 2 * HD, (jj + 1) * 2 * HD)
        fine = jnp.dot(fine_in, w2[:, h_cols], preferred_element_type=jnp.float32)
        hp[jj] = fine.astype(jnp.bfloat16)
    total = None
    for i in range(KCHUNKS):
        coarse_loads[i].wait()
        part = jnp.dot(
            p32[:, i * kdepth : (i + 1) * kdepth].astype(jnp.bfloat16),
            cw[i * kdepth : (i + 1) * kdepth, :],
            preferred_element_type=jnp.float32,
        )
        total = part if total is None else total + part
    for jj in range(per_plane):
        coarse = total[:, jj * 2 * HD : (jj + 1) * 2 * HD].astype(jnp.bfloat16)
        full = jnp.concatenate(
            [coarse, jnp.zeros((SLOTS - COARSE, 2 * HD), jnp.bfloat16)], axis=0
        )
        hp[jj] = jnp.where(level == 0, hp[jj], full)

    def slot_rows(index):
        return pl.ds(pl.multiple_of(index * SLOTS, SLOTS), SLOTS)

    def hist_copy(pj, slot):
        return pltpu.make_async_remote_copy(
            src_ref=hp.at[pj],
            dst_ref=hist.at[s, slot_rows(slot)],
            send_sem=hsend.at[pj],
            recv_sem=hrecv.at[slot],
            device_id=(pj * sibs + s, z),
            device_id_type=MESH,
        )

    for dj in range(1, per_plane):
        hist_copy(lax.rem(j + dj, per_plane), j).start()
    hist[s, slot_rows(j)] = hp[j]

    def plane_rows(pz):
        size = per_plane * local
        return pl.ds(pl.multiple_of(pz * size, size), size)

    def forward(pz, part, d):
        return pltpu.make_async_remote_copy(
            src_ref=kvbuf.at[part, plane_rows(pz)],
            dst_ref=kvbuf.at[part, plane_rows(pz)],
            send_sem=fsend.at[pz, d],
            recv_sem=frecv.at[part, pz],
            device_id=device(me, sib_of(d)),
            device_id_type=MESH,
        )

    def forward_hist(part, d):
        return pltpu.make_async_remote_copy(
            src_ref=hist.at[part],
            dst_ref=hist.at[part],
            send_sem=gsend.at[d],
            recv_sem=grecv.at[part],
            device_id=device(me, sib_of(d)),
            device_id_type=MESH,
        )

    for copy in own:
        copy.wait()
    for dz in [0] + z_order[:-1]:
        pz = lax.rem(z + dz, nz)
        for other, p in peers:
            if other == dz:
                for copy in qkv_in(p):
                    copy.wait_recv()
        loop(sibs - 1, lambda d: forward(pz, s, d).start())
    for dj in range(1, per_plane):
        pj = lax.rem(j + dj, per_plane)
        hist_copy(pj, pj).wait_recv()
    loop(sibs - 1, lambda d: forward_hist(s, d).start())

    factor = LOG2E / math.sqrt(HD)
    queries = HEADS * local

    def absorb(qb, pair, bias, first):
        rows = pl.ds(qb * QBLOCK, QBLOCK)
        scores = lax.dot_general(
            qbuf[rows],
            pair[:, :HD],
            (((1,), (1,)), ((), ())),
            preferred_element_type=jnp.float32,
        )
        if bias is not None:
            scores = scores + bias
        top = jnp.max(scores, axis=1, keepdims=True)
        if not first:
            old = m_ref[rows]
            top = jnp.maximum(old[:, :1], top)
        expo = jnp.exp2((scores - top) * factor)
        total = jnp.sum(expo, axis=1, keepdims=True)
        update = jnp.dot(
            expo.astype(jnp.bfloat16), pair[:, HD:], preferred_element_type=jnp.float32
        )
        wide = jnp.broadcast_to(top, (QBLOCK, HD))
        if first:
            l_ref[rows] = jnp.broadcast_to(total, (QBLOCK, HD))
            acc_ref[rows] = update
        else:
            shrink = jnp.exp2((old - wide) * factor)
            l_ref[rows] = l_ref[rows] * shrink + total
            acc_ref[rows] = acc_ref[rows] * shrink + update
        m_ref[rows] = wide

    def token_chunk(part, first):
        for qb in range(queries // QBLOCK):
            absorb(qb, kvbuf[part], None, first)

    def hist_bias(part):
        index = lax.broadcasted_iota(jnp.int32, (1, SLOTS), 1)
        pieces = []
        for jj in range(per_plane):
            g = jj * sibs + part
            fine_rows = jnp.where(cnt_ref[g] > 2, SLOTS, SLOTS // 2)
            live = jnp.where(lev_ref[g] == 0, fine_rows, COARSE)
            pieces.append(jnp.where(index < live, 0.0, very_low))
        return jnp.concatenate(pieces, axis=1)

    def hist_chunk(part):
        bias = hist_bias(part)
        for qb in range(queries // QBLOCK):
            absorb(qb, hist[part], bias, False)

    token_chunk(s, True)
    hist_chunk(s)

    def rest(d):
        part = sib_of(d)
        for pz in range(nz):
            forward(pz, part, d).wait_recv()
        token_chunk(part, False)
        forward_hist(part, d).wait_recv()
        hist_chunk(part)

    loop(sibs - 1, rest)

    def out_copy(p, slot):
        return pltpu.make_async_remote_copy(
            src_ref=res.at[rows_of(p)],
            dst_ref=obuf.at[slot],
            send_sem=osend.at[p],
            recv_sem=orecv.at[slot],
            device_id=device(p, s),
            device_id_type=MESH,
        )

    res[...] = (acc_ref[...] / l_ref[...]).astype(jnp.bfloat16)
    for _, p in peers:
        out_copy(p, me).start()
    obuf[me] = res[rows_of(me)]
    for _, p in peers:
        out_copy(p, p).wait_recv()
    for h in range(HEADS):
        out_ref[:, h * HD : (h + 1) * HD] = obuf[h]

    for _, p in peers:
        for copy in qkv(p):
            copy.wait_send()
        out_copy(p, me).wait_send()
    for dj in range(1, per_plane):
        hist_copy(lax.rem(j + dj, per_plane), j).wait_send()
    for pz in range(nz):
        loop(sibs - 1, lambda d: forward(pz, s, d).wait_send())
    loop(sibs - 1, lambda d: forward_hist(s, d).wait_send())


def body(nz, tm, queries, keys, values, history, fine_proj, coarse_proj, frame_counts, levels):
    local, width = queries.shape
    per_plane = HEADS // nz
    sibs = tm // per_plane
    heads_width = fine_proj.shape[1]
    bf16, f32 = jnp.bfloat16, jnp.float32
    rows = HEADS * local
    dma = pltpu.SemaphoreType.DMA
    others = max(sibs - 1, 1)
    return pl.pallas_call(
        functools.partial(kernel, nz, tm),
        out_shape=jax.ShapeDtypeStruct((local, width), bf16),
        in_specs=[pl.BlockSpec(memory_space=pl.ANY)] * 6
        + [pl.BlockSpec(memory_space=pltpu.SMEM)] * 2,
        out_specs=pl.BlockSpec(memory_space=pltpu.VMEM),
        scratch_shapes=[
            pltpu.VMEM((rows, HD), bf16),
            pltpu.VMEM((sibs, rows, 2 * HD), bf16),
            pltpu.VMEM((sibs, per_plane * SLOTS, 2 * HD), bf16),
            pltpu.VMEM((per_plane, SLOTS, 2 * HD), bf16),
            pltpu.VMEM((FRAMES, ROWS, LANES), bf16),
            pltpu.VMEM((FRAMES, LANES // HD, ROWS, HD), f32),
            pltpu.VMEM((COARSE, coarse_proj.shape[0]), f32),
            pltpu.VMEM((2 * fine_proj.shape[0], heads_width), bf16),
            pltpu.VMEM(coarse_proj.shape, bf16),
            pltpu.VMEM((rows, HD), bf16),
            pltpu.VMEM((HEADS, local, HD), bf16),
            pltpu.VMEM((rows, HD), f32),
            pltpu.VMEM((rows, HD), f32),
            pltpu.VMEM((rows, HD), f32),
            dma((HEADS, 3)),
            dma((HEADS, 3)),
            dma((3,)),
            dma((nz, others)),
            dma((sibs, nz)),
            dma((per_plane,)),
            dma((per_plane,)),
            dma((others,)),
            dma((sibs,)),
            dma((HEADS,)),
            dma((HEADS,)),
            dma((KCHUNKS,)),
            dma((8, 2)),
            dma(()),
        ],
        compiler_params=pltpu.CompilerParams(
            collective_id=0, has_side_effects=True, vmem_limit_bytes=56 * 1024 * 1024
        ),
        cost_estimate=pl.CostEstimate(
            flops=700_000_000, bytes_accessed=12_000_000, transcendentals=1_100_000
        ),
    )(queries, keys, values, history, fine_proj, coarse_proj, frame_counts, levels)


def solution(mesh):
    in_specs = (
        P(("tm", "head"), None),
        P(("tm", "head"), None),
        P(("tm", "head"), None),
        P("tm", None, None, None),
        P(None, "head"),
        P(None, "head"),
        P(),
        P(),
    )
    out_specs = P(("tm", "head"), None)
    nz, tm = mesh.shape["head"], mesh.shape["tm"]
    return jax.shard_map(
        functools.partial(body, nz, tm),
        mesh=mesh,
        in_specs=in_specs,
        out_specs=out_specs,
        check_vma=False,
    )
```

time: 103 us -> 30.8 us (0.30)
  waiting for transfers between devices: 32.2 us -> 0 us
  Pallas kernels: 0 us -> 29.1 us
  local copies, waits for them, and re-layouts: 20.7 us -> 1.57 us
  between operations: 14.2 us -> 0.01 us
  starting transfers between devices: 11.4 us -> 0 us
  blocking collectives: 10.7 us -> 0 us
  matrix products: 8.81 us -> 0 us
  other arithmetic: 5.1 us -> 0 us
    pallas_call x0 -> x1, Pallas kernels: none -> 29.1 us  [body(): pl.pallas_call(functools.partial(kernel, nz, tm), out_shape=jax.ShapeDtyp...]
    all_gather x1 -> x0, waiting for transfers between devices: 26.6 us -> none  [body(): piece = lax.all_gather(packed, 'tm', axis=0, tiled=True)]
    all_to_all x2 -> x0, starting transfers between devices: 11.4 us -> none  [the longest x1 6.32 us: body(): lax.all_to_all(pairs, 'head', split_axis=1, concat_axis=0, tiled=True)]
    all_to_all x1 -> x0, blocking collectives: 10.7 us -> none  [body(): lax.all_to_all(result, 'head', split_axis=0, concat_axis=1, tiled=True)]
    another operation x4 -> x0, local copies, waits for them, and re-layouts: 10.2 us -> none  [the longest x1 7.84 us: absorb_blocks(): pair_rows.reshape(steps_count, block, pair_rows.shape[1], pair_rows.shape...]
    dot_general x5 -> x0, matrix products: 8.81 us -> none  [the longest x1 4.58 us: coarse_only(): jnp.dot(coarse, coarse_proj, preferred_element_type=jnp.float32)]
    all_to_all x2 -> x0, waiting for transfers between devices: 5.56 us -> none  [the longest x1 5.55 us: body(): lax.all_to_all(queries, 'head', split_axis=1, concat_axis=0, tiled=True)]
    dynamic_slice x6 -> x0, local copies, waits for them, and re-layouts: 5.24 us -> none  [absorb_blocks(): running, unused = lax.scan(one_step, running, (stacked, masks))]
  transfers between devices with their start and end apart: 3 -> 0, of which waited for: 2 -> 0; matrix products, arithmetic and copies ran while one was open for 10% -> 0% of each run, Pallas kernels for 0% -> 0%
where the time goes in v1:
time: 30.8 us; the launch traced here: 30.6 us
  Pallas kernels  29.1 us (94%)
  local copies, waits for them, and re-layouts  1.57 us (5%)
    pallas_call x1, Pallas kernels, body(): pl.pallas_call(functools.partial(kernel, nz, tm), out_shape=jax.ShapeDtyp...  29.1 us
    unnamed x1, local copies, waits for them, and re-layouts  1.57 us

profile of v1, /device:TPU:0, one launch (start us, length us, event | category | flops | bytes accessed | tf_op | source)
XLA Modules:
  0.0 30.6 jit_solution(11375782756334031477)
XLA Ops:
  0.0 29.1 %shard_map.82 = bf16[32,2048]{1,0:T(8,128)(2,1)} custom-call(bf16[32,2048]{1,0:T(8,128)(2,1)} %q_ref.1, bf16[32,2048]{1,0:T(8,128)(2,1)} %k_ref.1, bf16[32,2048]{1,0:T(8,128)(2,1)} %v_ref.1, bf16[1,4,32,512]{3,2,1,0:T(8,128)(2,1)} %h_ref.1, bf16[512,1024]{1,0:T(8,128)(2,1)} %fw_ref.1, bf16[4096,1024]{1,0:T(8,128)(2,1)} %cw_ref.1, s32[8]{0:T(128)} %cnt_ref.1, ...), custom_call_target="tpu_custom_call" | custom-call | flops 700000000 | bytes 12000000 | tf_op jit(solution)/shard_map/pallas_call | solution.py:398
  29.1 1.6 %copy.10 = bf16[32,2048]{1,0:T(8,128)(2,1)} copy(bf16[32,2048]{1,0:T(8,128)(2,1)} %shard_map.82) | data formatting | bytes 262144

commit v2 on v1

--- a/solution.py
+++ b/solution.py
@@ -48,8 +48,9 @@
     cnt_ref,
     lev_ref,
     out_ref,
-    qbuf,
-    kvbuf,
+    inbuf,
+    pack,
+    recv,
     hist,
     hp,
     hv,
@@ -64,7 +65,7 @@
     acc_ref,
     send_sem,
     recv_sem,
-    own_sem,
+    in_sem,
     fsend,
     frecv,
     hsend,
@@ -87,7 +88,13 @@
     me = z * per_plane + j
     kdepth = cw.shape[0] // KCHUNKS
 
+    in_loads = [
+        pltpu.make_async_copy(src, inbuf.at[n], in_sem.at[n])
+        for n, src in enumerate((q_ref, k_ref, v_ref))
+    ]
     hist_load = pltpu.make_async_copy(h_ref.at[0], hv, hsem)
+    for load in in_loads:
+        load.start()
     hist_load.start()
     fine_loads = []
     for i in range(8):
@@ -133,56 +140,28 @@
         load.start()
     for load in coarse_loads:
         load.start()
+    for n, load in enumerate(in_loads):
+        load.wait()
+        for h in range(HEADS):
+            pack[h, n * local : (n + 1) * local, :] = inbuf[n, :, h * HD : (h + 1) * HD]
     pl.semaphore_wait(barrier, HEADS - 1 + sibs - 1)
-
-    def columns(head):
-        return pl.ds(pl.multiple_of(head * HD, HD), HD)
 
     def rows_of(head):
         return pl.ds(pl.multiple_of(head * local, local), local)
 
-    def targets(row):
-        return (
-            qbuf.at[rows_of(row)],
-            kvbuf.at[s, rows_of(row), pl.ds(0, HD)],
-            kvbuf.at[s, rows_of(row), pl.ds(HD, HD)],
-        )
-
-    def qkv(p):
-        return [
-            pltpu.make_async_remote_copy(
-                src_ref=src.at[:, columns(p)],
-                dst_ref=dst,
-                send_sem=send_sem.at[p, n],
-                recv_sem=recv_sem.at[me, n],
-                device_id=device(p, s),
-                device_id_type=MESH,
-            )
-            for n, (src, dst) in enumerate(zip((q_ref, k_ref, v_ref), targets(me)))
-        ]
-
-    def qkv_in(p):
-        return [
-            pltpu.make_async_remote_copy(
-                src_ref=src.at[:, columns(p)],
-                dst_ref=dst,
-                send_sem=send_sem.at[p, n],
-                recv_sem=recv_sem.at[p, n],
-                device_id=device(p, s),
-                device_id_type=MESH,
-            )
-            for n, (src, dst) in enumerate(zip((q_ref, k_ref, v_ref), targets(p)))
-        ]
+    def qkv(p, slot):
+        return pltpu.make_async_remote_copy(
+            src_ref=pack.at[p],
+            dst_ref=recv.at[s, slot],
+            send_sem=send_sem.at[p],
+            recv_sem=recv_sem.at[slot],
+            device_id=device(p, s),
+            device_id_type=MESH,
+        )
 
     for _, p in peers:
-        for copy in qkv(p):
-            copy.start()
-    own = [
-        pltpu.make_async_copy(src.at[:, columns(me)], dst, own_sem.at[n])
-        for n, (src, dst) in enumerate(zip((q_ref, k_ref, v_ref), targets(me)))
-    ]
-    for copy in own:
-        copy.start()
+        qkv(p, me).start()
+    recv[s, me] = pack[me]
 
     count = cnt_ref[t]
     level = lev_ref[t]
@@ -254,14 +233,13 @@
         hist_copy(lax.rem(j + dj, per_plane), j).start()
     hist[s, slot_rows(j)] = hp[j]
 
-    def plane_rows(pz):
-        size = per_plane * local
-        return pl.ds(pl.multiple_of(pz * size, size), size)
-
     def forward(pz, part, d):
+        block = recv.at[
+            part, pl.ds(pz * per_plane, per_plane), pl.ds(local, 2 * local)
+        ]
         return pltpu.make_async_remote_copy(
-            src_ref=kvbuf.at[part, plane_rows(pz)],
-            dst_ref=kvbuf.at[part, plane_rows(pz)],
+            src_ref=block,
+            dst_ref=block,
             send_sem=fsend.at[pz, d],
             recv_sem=frecv.at[part, pz],
             device_id=device(me, sib_of(d)),
@@ -278,14 +256,11 @@
             device_id_type=MESH,
         )
 
-    for copy in own:
-        copy.wait()
     for dz in [0] + z_order[:-1]:
         pz = lax.rem(z + dz, nz)
         for other, p in peers:
             if other == dz:
-                for copy in qkv_in(p):
-                    copy.wait_recv()
+                qkv(p, p).wait_recv()
         loop(sibs - 1, lambda d: forward(pz, s, d).start())
     for dj in range(1, per_plane):
         pj = lax.rem(j + dj, per_plane)
@@ -295,11 +270,16 @@
     factor = LOG2E / math.sqrt(HD)
     queries = HEADS * local
 
-    def absorb(qb, pair, bias, first):
+    def queries_in(qb):
+        heads = QBLOCK // local
+        block = recv[s, qb * heads : (qb + 1) * heads, 0:local, :]
+        return block.reshape(QBLOCK, HD)
+
+    def absorb(qb, keys, values, bias, first):
         rows = pl.ds(qb * QBLOCK, QBLOCK)
         scores = lax.dot_general(
-            qbuf[rows],
-            pair[:, :HD],
+            queries_in(qb),
+            keys,
             (((1,), (1,)), ((), ())),
             preferred_element_type=jnp.float32,
         )
@@ -312,7 +292,7 @@
         expo = jnp.exp2((scores - top) * factor)
         total = jnp.sum(expo, axis=1, keepdims=True)
         update = jnp.dot(
-            expo.astype(jnp.bfloat16), pair[:, HD:], preferred_element_type=jnp.float32
+            expo.astype(jnp.bfloat16), values, preferred_element_type=jnp.float32
         )
         wide = jnp.broadcast_to(top, (QBLOCK, HD))
         if first:
@@ -325,8 +305,10 @@
         m_ref[rows] = wide
 
     def token_chunk(part, first):
+        keys = recv[part, :, local : 2 * local, :].reshape(queries, HD)
+        values = recv[part, :, 2 * local : 3 * local, :].reshape(queries, HD)
         for qb in range(queries // QBLOCK):
-            absorb(qb, kvbuf[part], None, first)
+            absorb(qb, keys, values, None, first)
 
     def hist_bias(part):
         index = lax.broadcasted_iota(jnp.int32, (1, SLOTS), 1)
@@ -341,7 +323,7 @@
     def hist_chunk(part):
         bias = hist_bias(part)
         for qb in range(queries // QBLOCK):
-            absorb(qb, hist[part], bias, False)
+            absorb(qb, hist[part, :, :HD], hist[part, :, HD:], bias, False)
 
     token_chunk(s, True)
     hist_chunk(s)
@@ -376,8 +358,7 @@
         out_ref[:, h * HD : (h + 1) * HD] = obuf[h]
 
     for _, p in peers:
-        for copy in qkv(p):
-            copy.wait_send()
+        qkv(p, me).wait_send()
         out_copy(p, me).wait_send()
     for dj in range(1, per_plane):
         hist_copy(lax.rem(j + dj, per_plane), j).wait_send()
@@ -397,13 +378,14 @@
     others = max(sibs - 1, 1)
     return pl.pallas_call(
         functools.partial(kernel, nz, tm),
-        out_shape=jax.ShapeDtypeStruct((local, width), bf16),
+        out_shape=pltpu.VMEM((local, width), bf16),
         in_specs=[pl.BlockSpec(memory_space=pl.ANY)] * 6
         + [pl.BlockSpec(memory_space=pltpu.SMEM)] * 2,
         out_specs=pl.BlockSpec(memory_space=pltpu.VMEM),
         scratch_shapes=[
-            pltpu.VMEM((rows, HD), bf16),
-            pltpu.VMEM((sibs, rows, 2 * HD), bf16),
+            pltpu.VMEM((3, local, width), bf16),
+            pltpu.VMEM((HEADS, 3 * local, HD), bf16),
+            pltpu.VMEM((sibs, HEADS, 3 * local, HD), bf16),
             pltpu.VMEM((sibs, per_plane * SLOTS, 2 * HD), bf16),
             pltpu.VMEM((per_plane, SLOTS, 2 * HD), bf16),
             pltpu.VMEM((FRAMES, ROWS, LANES), bf16),
@@ -416,8 +398,8 @@
             pltpu.VMEM((rows, HD), f32),
             pltpu.VMEM((rows, HD), f32),
             pltpu.VMEM((rows, HD), f32),
-            dma((HEADS, 3)),
-            dma((HEADS, 3)),
+            dma((HEADS,)),
+            dma((HEADS,)),
             dma((3,)),
             dma((nz, others)),
             dma((sibs, nz)),

time: 30.8 us -> 28.4 us (0.922)
  Pallas kernels: 29.1 us -> 27.6 us
  local copies, waits for them, and re-layouts: 1.57 us -> 0.66 us
    pallas_call x1, Pallas kernels: 29.1 us -> 27.6 us  [body(): pl.pallas_call(functools.partial(kernel, nz, tm), out_shape=pltpu.VMEM((l...]
    unnamed x1, local copies, waits for them, and re-layouts: 1.57 us -> 0.66 us
where the time goes in v2:
time: 28.4 us; the launch traced here: 28.2 us
  Pallas kernels  27.6 us (97%)
  local copies, waits for them, and re-layouts  0.66 us (2%)
    pallas_call x1, Pallas kernels, body(): pl.pallas_call(functools.partial(kernel, nz, tm), out_shape=pltpu.VMEM((l...  27.6 us
    unnamed x1, local copies, waits for them, and re-layouts  0.66 us

profile of v2, /device:TPU:0, one launch (start us, length us, event | category | flops | bytes accessed | tf_op | source)
XLA Modules:
  0.0 28.2 jit_solution(9482269965853964216)
XLA Ops:
  0.0 27.6 %shard_map.82 = bf16[32,2048]{1,0:T(8,128)(2,1)S(1)} custom-call(bf16[32,2048]{1,0:T(8,128)(2,1)} %q_ref.1, bf16[32,2048]{1,0:T(8,128)(2,1)} %k_ref.1, bf16[32,2048]{1,0:T(8,128)(2,1)} %v_ref.1, bf16[1,4,32,512]{3,2,1,0:T(8,128)(2,1)} %h_ref.1, bf16[512,1024]{1,0:T(8,128)(2,1)} %fw_ref.1, bf16[4096,1024]{1,0:T(8,128)(2,1)} %cw_ref.1, s32[8]{0:T(128)} %cnt_ref.1, ...), custom_call_target="tpu_custom_call" | custom-call | flops 700000000 | bytes 12000000 | tf_op jit(solution)/shard_map/pallas_call | solution.py:379
  27.6 0.7 %copy.10 = bf16[32,2048]{1,0:T(8,128)(2,1)} copy(bf16[32,2048]{1,0:T(8,128)(2,1)S(1)} %shard_map.82) | data formatting | bytes 262144

commit v3 on v2

--- a/solution.py
+++ b/solution.py
@@ -16,7 +16,6 @@
 SLOTS = 128
 COARSE = 16
 KCHUNKS = 4
-QBLOCK = 256
 
 very_low = -1e30
 LOG2E = 1.4426950408889634
@@ -117,19 +116,18 @@
         plane = lax.div(head, per_plane)
         return (lax.rem(head, per_plane) * sibs + sib, plane)
 
-    z_order = sorted(range(nz), key=lambda d: -min(d, nz - d))
-    peers = []
-    for dz in z_order:
-        for dj in range(per_plane):
-            if dz or dj:
-                pz = lax.rem(z + dz, nz)
-                peers.append((dz, pz * per_plane + lax.rem(j + dj, per_plane)))
+    half = HEADS // 2
+    near = lax.div(me, half)
+    far = 1 - near
+    far_peers = [far * half + lax.rem(me + i, half) for i in range(half)]
+    near_peers = [near * half + lax.rem(me + i, half) for i in range(1, half)]
+    peers = far_peers + near_peers
 
     def sib_of(d):
         return lax.rem(s + 1 + d, sibs)
 
     barrier = pltpu.get_barrier_semaphore()
-    for _, p in peers:
+    for p in peers:
         pl.semaphore_signal(barrier, inc=1, device_id=device(p, s), device_id_type=MESH)
 
     def greet(d):
@@ -159,7 +157,7 @@
             device_id_type=MESH,
         )
 
-    for _, p in peers:
+    for p in peers:
         qkv(p, me).start()
     recv[s, me] = pack[me]
 
@@ -233,15 +231,15 @@
         hist_copy(lax.rem(j + dj, per_plane), j).start()
     hist[s, slot_rows(j)] = hp[j]
 
-    def forward(pz, part, d):
+    def forward(side, part, d):
         block = recv.at[
-            part, pl.ds(pz * per_plane, per_plane), pl.ds(local, 2 * local)
+            part, pl.ds(side * half, half), pl.ds(local, 2 * local)
         ]
         return pltpu.make_async_remote_copy(
             src_ref=block,
             dst_ref=block,
-            send_sem=fsend.at[pz, d],
-            recv_sem=frecv.at[part, pz],
+            send_sem=fsend.at[side, d],
+            recv_sem=frecv.at[part, side],
             device_id=device(me, sib_of(d)),
             device_id_type=MESH,
         )
@@ -256,27 +254,16 @@
             device_id_type=MESH,
         )
 
-    for dz in [0] + z_order[:-1]:
-        pz = lax.rem(z + dz, nz)
-        for other, p in peers:
-            if other == dz:
-                qkv(p, p).wait_recv()
-        loop(sibs - 1, lambda d: forward(pz, s, d).start())
-    for dj in range(1, per_plane):
-        pj = lax.rem(j + dj, per_plane)
-        hist_copy(pj, pj).wait_recv()
-    loop(sibs - 1, lambda d: forward_hist(s, d).start())
-
     factor = LOG2E / math.sqrt(HD)
     queries = HEADS * local
+    block_rows = half * local
 
     def queries_in(qb):
-        heads = QBLOCK // local
-        block = recv[s, qb * heads : (qb + 1) * heads, 0:local, :]
-        return block.reshape(QBLOCK, HD)
+        block = recv[s, pl.ds(qb * half, half), 0:local, :]
+        return block.reshape(block_rows, HD)
 
     def absorb(qb, keys, values, bias, first):
-        rows = pl.ds(qb * QBLOCK, QBLOCK)
+        rows = pl.ds(pl.multiple_of(qb * block_rows, block_rows), block_rows)
         scores = lax.dot_general(
             queries_in(qb),
             keys,
@@ -294,9 +281,9 @@
         update = jnp.dot(
             expo.astype(jnp.bfloat16), values, preferred_element_type=jnp.float32
         )
-        wide = jnp.broadcast_to(top, (QBLOCK, HD))
+        wide = jnp.broadcast_to(top, (block_rows, HD))
         if first:
-            l_ref[rows] = jnp.broadcast_to(total, (QBLOCK, HD))
+            l_ref[rows] = jnp.broadcast_to(total, (block_rows, HD))
             acc_ref[rows] = update
         else:
             shrink = jnp.exp2((old - wide) * factor)
@@ -304,11 +291,10 @@
             acc_ref[rows] = acc_ref[rows] * shrink + update
         m_ref[rows] = wide
 
-    def token_chunk(part, first):
+    def token_chunk(qb, part):
         keys = recv[part, :, local : 2 * local, :].reshape(queries, HD)
         values = recv[part, :, 2 * local : 3 * local, :].reshape(queries, HD)
-        for qb in range(queries // QBLOCK):
-            absorb(qb, keys, values, None, first)
+        absorb(qb, keys, values, None, False)
 
     def hist_bias(part):
         index = lax.broadcasted_iota(jnp.int32, (1, SLOTS), 1)
@@ -320,23 +306,9 @@
             pieces.append(jnp.where(index < live, 0.0, very_low))
         return jnp.concatenate(pieces, axis=1)
 
-    def hist_chunk(part):
+    def hist_chunk(qb, part, first):
         bias = hist_bias(part)
-        for qb in range(queries // QBLOCK):
-            absorb(qb, hist[part, :, :HD], hist[part, :, HD:], bias, False)
-
-    token_chunk(s, True)
-    hist_chunk(s)
-
-    def rest(d):
-        part = sib_of(d)
-        for pz in range(nz):
-            forward(pz, part, d).wait_recv()
-        token_chunk(part, False)
-        forward_hist(part, d).wait_recv()
-        hist_chunk(part)
-
-    loop(sibs - 1, rest)
+        absorb(qb, hist[part, :, :HD], hist[part, :, HD:], bias, first)
 
     def out_copy(p, slot):
         return pltpu.make_async_remote_copy(
@@ -348,22 +320,59 @@
             device_id_type=MESH,
         )
 
-    res[...] = (acc_ref[...] / l_ref[...]).astype(jnp.bfloat16)
-    for _, p in peers:
-        out_copy(p, me).start()
+    def finish(qb, heads):
+        rows = pl.ds(pl.multiple_of(qb * block_rows, block_rows), block_rows)
+        res[rows] = (acc_ref[rows] / l_ref[rows]).astype(jnp.bfloat16)
+        for p in heads:
+            out_copy(p, me).start()
+
+    for p in near_peers:
+        qkv(p, p).wait_recv()
+    loop(sibs - 1, lambda d: forward(near, s, d).start())
+    for dj in range(1, per_plane):
+        pj = lax.rem(j + dj, per_plane)
+        hist_copy(pj, pj).wait_recv()
+    loop(sibs - 1, lambda d: forward_hist(s, d).start())
+    hist_chunk(near, s, True)
+    for p in far_peers:
+        qkv(p, p).wait_recv()
+    loop(sibs - 1, lambda d: forward(far, s, d).start())
+
+    hist_chunk(far, s, True)
+    token_chunk(far, s)
+
+    def far_rest(d):
+        part = sib_of(d)
+        forward_hist(part, d).wait_recv()
+        hist_chunk(far, part, False)
+        for side in range(2):
+            forward(side, part, d).wait_recv()
+        token_chunk(far, part)
+
+    loop(sibs - 1, far_rest)
+    finish(far, far_peers)
+    token_chunk(near, s)
+
+    def near_rest(d):
+        part = sib_of(d)
+        hist_chunk(near, part, False)
+        token_chunk(near, part)
+
+    loop(sibs - 1, near_rest)
+    finish(near, near_peers)
     obuf[me] = res[rows_of(me)]
-    for _, p in peers:
+    for p in peers:
         out_copy(p, p).wait_recv()
     for h in range(HEADS):
         out_ref[:, h * HD : (h + 1) * HD] = obuf[h]
 
-    for _, p in peers:
+    for p in peers:
         qkv(p, me).wait_send()
         out_copy(p, me).wait_send()
     for dj in range(1, per_plane):
         hist_copy(lax.rem(j + dj, per_plane), j).wait_send()
-    for pz in range(nz):
-        loop(sibs - 1, lambda d: forward(pz, s, d).wait_send())
+    for side in range(2):
+        loop(sibs - 1, lambda d: forward(side, s, d).wait_send())
     loop(sibs - 1, lambda d: forward_hist(s, d).wait_send())
 
 
@@ -401,8 +410,8 @@
             dma((HEADS,)),
             dma((HEADS,)),
             dma((3,)),
-            dma((nz, others)),
-            dma((sibs, nz)),
+            dma((2, others)),
+            dma((sibs, 2)),
             dma((per_plane,)),
             dma((per_plane,)),
             dma((others,)),

time: 28.4 us -> 27.5 us (0.968)
  Pallas kernels: 27.6 us -> 26.6 us
    pallas_call x1, Pallas kernels: 27.6 us -> 26.6 us  [body(): pl.pallas_call(functools.partial(kernel, nz, tm), out_shape=pltpu.VMEM((l...]
where the time goes in v3:
time: 27.5 us; the launch traced here: 27.3 us
  Pallas kernels  26.6 us (97%)
  local copies, waits for them, and re-layouts  0.66 us (2%)
    pallas_call x1, Pallas kernels, body(): pl.pallas_call(functools.partial(kernel, nz, tm), out_shape=pltpu.VMEM((l...  26.6 us
    unnamed x1, local copies, waits for them, and re-layouts  0.66 us

profile of v3, /device:TPU:0, one launch (start us, length us, event | category | flops | bytes accessed | tf_op | source)
XLA Modules:
  0.0 27.3 jit_solution(5902588158819760651)
XLA Ops:
  0.0 26.6 %shard_map.82 = bf16[32,2048]{1,0:T(8,128)(2,1)S(1)} custom-call(bf16[32,2048]{1,0:T(8,128)(2,1)} %q_ref.1, bf16[32,2048]{1,0:T(8,128)(2,1)} %k_ref.1, bf16[32,2048]{1,0:T(8,128)(2,1)} %v_ref.1, bf16[1,4,32,512]{3,2,1,0:T(8,128)(2,1)} %h_ref.1, bf16[512,1024]{1,0:T(8,128)(2,1)} %fw_ref.1, bf16[4096,1024]{1,0:T(8,128)(2,1)} %cw_ref.1, s32[8]{0:T(128)} %cnt_ref.1, ...), custom_call_target="tpu_custom_call" | custom-call | flops 700000000 | bytes 12000000 | tf_op jit(solution)/shard_map/pallas_call | solution.py:388
  26.6 0.7 %copy.10 = bf16[32,2048]{1,0:T(8,128)(2,1)} copy(bf16[32,2048]{1,0:T(8,128)(2,1)S(1)} %shard_map.82) | data formatting | bytes 262144

commit v4 on v3

--- a/solution.py
+++ b/solution.py
@@ -334,6 +334,13 @@
         hist_copy(pj, pj).wait_recv()
     loop(sibs - 1, lambda d: forward_hist(s, d).start())
     hist_chunk(near, s, True)
+
+    def near_history(d):
+        part = sib_of(d)
+        forward_hist(part, d).wait_recv()
+        hist_chunk(near, part, False)
+
+    loop(sibs - 1, near_history)
     for p in far_peers:
         qkv(p, p).wait_recv()
     loop(sibs - 1, lambda d: forward(far, s, d).start())
@@ -343,7 +350,6 @@
 
     def far_rest(d):
         part = sib_of(d)
-        forward_hist(part, d).wait_recv()
         hist_chunk(far, part, False)
         for side in range(2):
             forward(side, part, d).wait_recv()
@@ -354,9 +360,7 @@
     token_chunk(near, s)
 
     def near_rest(d):
-        part = sib_of(d)
-        hist_chunk(near, part, False)
-        token_chunk(near, part)
+        token_chunk(near, sib_of(d))
 
     loop(sibs - 1, near_rest)
     finish(near, near_peers)

time: 27.5 us -> 28 us (1.018)
  Pallas kernels: 26.6 us -> 27.2 us
    pallas_call x1, Pallas kernels: 26.6 us -> 27.2 us  [body(): pl.pallas_call(functools.partial(kernel, nz, tm), out_shape=pltpu.VMEM((l...]
where the time goes in v4:
time: 28 us; the launch traced here: 27.8 us
  Pallas kernels  27.2 us (97%)
  local copies, waits for them, and re-layouts  0.66 us (2%)
    pallas_call x1, Pallas kernels, body(): pl.pallas_call(functools.partial(kernel, nz, tm), out_shape=pltpu.VMEM((l...  27.2 us
    unnamed x1, local copies, waits for them, and re-layouts  0.66 us

profile of v4, /device:TPU:0, one launch (start us, length us, event | category | flops | bytes accessed | tf_op | source)
XLA Modules:
  0.0 27.8 jit_solution(5434213424809527433)
XLA Ops:
  0.0 27.2 %shard_map.82 = bf16[32,2048]{1,0:T(8,128)(2,1)S(1)} custom-call(bf16[32,2048]{1,0:T(8,128)(2,1)} %q_ref.1, bf16[32,2048]{1,0:T(8,128)(2,1)} %k_ref.1, bf16[32,2048]{1,0:T(8,128)(2,1)} %v_ref.1, bf16[1,4,32,512]{3,2,1,0:T(8,128)(2,1)} %h_ref.1, bf16[512,1024]{1,0:T(8,128)(2,1)} %fw_ref.1, bf16[4096,1024]{1,0:T(8,128)(2,1)} %cw_ref.1, s32[8]{0:T(128)} %cnt_ref.1, ...), custom_call_target="tpu_custom_call" | custom-call | flops 700000000 | bytes 12000000 | tf_op jit(solution)/shard_map/pallas_call | solution.py:392
  27.2 0.7 %copy.10 = bf16[32,2048]{1,0:T(8,128)(2,1)} copy(bf16[32,2048]{1,0:T(8,128)(2,1)S(1)} %shard_map.82) | data formatting | bytes 262144
